TPU v7x, 512 devices: a whole 4x4x16 slice. The times are simulated.
512 devices in a mesh: section: 8 (over x, core), expert: 8 (over z_lo), dp: 8 (over y, z_hi).
Axes of the slice: x: 4, y: 4, z: 16 (z_hi: 2, z_lo: 8; z = z_hi * 8 + z_lo), core: 2. Of those that a mesh axis runs over, the one named last changes fastest.
Arguments:
- layer_input: bfloat16 [8, 8192, 2048], P('section', ('expert', 'dp')), may hold values from -6 to 6
- output_grad: bfloat16 [8, 8192, 2048], P('section', ('expert', 'dp')), may hold values from -6 to 6
- expert_ids: int32 [8, 8192], P('section', ('expert', 'dp')), may hold values from 0 to 63, as said below
- w_gate: bfloat16 [8, 2048, 8192], P('section', None, ('expert', 'dp')), may hold values from -0.125 to 0.125
- w_up: bfloat16 [8, 2048, 8192], P('section', None, ('expert', 'dp')), may hold values from -0.125 to 0.125
- w_down: bfloat16 [8, 2048, 8192], P('section', None, ('expert', 'dp')), may hold values from -0.0625 to 0.0625
Outputs:
- input_grad: bfloat16 [8, 8192, 2048], P('section', ('expert', 'dp'))
- grad_gate: bfloat16 [8, 2048, 8192], P('section', None, ('expert', 'dp'))
- grad_up: bfloat16 [8, 2048, 8192], P('section', None, ('expert', 'dp'))
- grad_down: bfloat16 [8, 2048, 8192], P('section', None, ('expert', 'dp'))
Inputs may be any that keep to these rules, and one draw needn't show every extreme that they name: `expert_ids`: expert 0 is the expert of these weights. Every device's 128 tokens name expert 0 between 1 and 8 times, and on every section some device names it exactly 8 times.
All inputs are finite; a program needn't handle non-finite values.
Results may differ from a plain program's by a relative error of at most 0.0065.
Values may be sent and summed in bfloat16 or wider, within the bound.
A program may use at most 64 MiB of HBM per device.

v0:
```python
import jax
import jax.numpy as jnp
from jax import lax
from jax.sharding import PartitionSpec as P

SLOT = 8
GROUP = ("expert", "dp")


def shifted(value, axis, steps):
    count = lax.axis_size(axis)
    pairs = [(source, (source + steps) % count) for source in range(count)]
    return lax.ppermute(value, axis, pairs)


def body(layer_input, output_grad, expert_ids, w_gate, w_up, w_down):
    inputs = layer_input[0]
    grads = output_grad[0]
    routes = expert_ids[0]
    chosen = (routes == 0).astype(jnp.int32)
    order = jnp.arange(chosen.shape[0], dtype=jnp.int32)
    within = jnp.sum(jnp.where(order[None, :] < order[:, None], chosen[None, :], 0), axis=1)
    target = jnp.where(chosen > 0, within, SLOT)
    places = jnp.arange(SLOT, dtype=jnp.int32)
    match = (target[None, :] == places[:, None]).astype(jnp.bfloat16)
    send_x = jnp.dot(match, inputs, preferred_element_type=jnp.float32).astype(jnp.bfloat16)
    send_dy = jnp.dot(match, grads, preferred_element_type=jnp.float32).astype(jnp.bfloat16)
    moved_grads = shifted(grads, "section", -1)
    moved_match = shifted(match, "section", -1)
    rows = lax.all_gather(jnp.stack([send_x, send_dy]), GROUP, axis=1, tiled=True)
    x_rows, dy_rows = (rows[0], rows[1])
    w_both = jnp.concatenate([w_gate[0], w_up[0]], axis=1)
    both = jnp.dot(x_rows, w_both, preferred_element_type=jnp.float32)
    width = w_gate.shape[2]
    gate, upper = (both[:, :width], both[:, width:])
    sigma = jax.nn.sigmoid(gate)
    active = gate * sigma
    hidden = (active * upper).astype(jnp.bfloat16)
    d_hidden = jnp.dot(dy_rows, w_down[0], preferred_element_type=jnp.float32)
    d_gate = (d_hidden * upper * sigma * (1.0 + gate * (1.0 - sigma))).astype(jnp.bfloat16)
    d_up = (d_hidden * active).astype(jnp.bfloat16)
    d_both = jnp.concatenate([d_gate, d_up], axis=1)
    back_dims = (((1,), (1,)), ((), ()))
    d_part = lax.dot_general(d_both, w_both, back_dims, preferred_element_type=jnp.float32)
    d_rows = lax.psum_scatter(d_part.astype(jnp.bfloat16), GROUP, scatter_dimension=0, tiled=True)
    d_rows = shifted(d_rows, "section", -1)
    row_dims = (((0,), (0,)), ((), ()))
    part_both = lax.dot_general(
        x_rows, d_both, row_dims, preferred_element_type=jnp.float32
    ).astype(jnp.bfloat16)
    part_down = lax.dot_general(
        dy_rows, hidden, row_dims, preferred_element_type=jnp.float32
    ).astype(jnp.bfloat16)
    term = lax.dot_general(
        moved_match, d_rows, (((0,), (0,)), ((), ())), preferred_element_type=jnp.float32
    )
    token_grad = (moved_grads.astype(jnp.float32) + term).astype(jnp.bfloat16)
    return (
        token_grad[None],
        part_both[None, :, :width],
        part_both[None, :, width:],
        part_down[None],
    )


def solution(mesh):
    rows = P("section", ("expert", "dp"), None)
    weights = P("section", None, ("expert", "dp"))
    in_specs = (rows, rows, P("section", ("expert", "dp")), weights, weights, weights)
    out_specs = (rows, weights, weights, weights)
    return jax.shard_map(body, mesh=mesh, in_specs=in_specs, out_specs=out_specs, check_vma=False)
```

profile of v0, /device:TPU:65, one launch (start us, length us, event | category | flops | bytes accessed | tf_op | source)
XLA Modules:
  0.0 1204.5 jit_solution(17072513962563415594)
XLA Ops:
  7.2 0.0 copy-start
  7.2 0.0 all-gather.2.cloned.1.call-start
  7.2 0.7 fusion.14
  7.9 0.1 select_reduce_fusion
  8.0 0.7 fusion.13
  8.7 1.2 fusion.2
  9.9 1.2 fusion.1
  11.2 0.6 pad_maximum_fusion.6
  11.8 0.0 all-gather.2.cloned.1.call-update
  11.8 0.0 reduce-scatter.2.cloned.1.call-start
  11.9 588.9 %all-gather.2.cloned.1.call-done = bf16[2,512,2048]{2,1,0:T(8,128)(2,1)} async-done(((bf16[2,8,2048]{2,1,0:T(8,128)(2,1)}), bf16[2,512,2048]{2,1,0:T(8,128)(2,1)}) %all-gather.2.cloned.1.call-update) | async-done | bytes 4194320 | tf_op jit(solution)/shard_map/all_gather | solution.py:30
  600.8 0.0 copy-start.4
  600.8 2.7 fusion.4
  603.5 0.0 copy-done
  603.5 0.4 copy-done.4
  603.9 0.0 copy-start.1
  603.9 0.0 copy-start.2
  603.9 0.9 multiply_convert_fusion.2
  604.8 0.2 copy-done.1
  605.0 0.2 copy-done.2
  605.1 2.1 convolution_convert_fusion
  607.2 0.0 copy-start.3
  607.2 0.0 reduce-scatter.2.cloned.1.call-update
  607.3 48.0 %collective-permute-start.1 = (bf16[8,128]{1,0:T(8,128)(2,1)S(1)}, bf16[8,128]{1,0:T(8,128)(2,1)S(1)}, u32[]{:S(2)}, u32[]{:S(2)}) collective-permute-start(bf16[8,128]{1,0:T(8,128)(2,1)S(1)} %fusion.10), channel_id=1, source_target_pairs={{0,448},{64,0},{128,64},{192,128},{256,192},{320,256},{384,320},{4... | collective-permute-start | bytes 6152 | tf_op jit(solution)/shard_map/ppermute | solution.py:13
  655.2 0.0 copy-done.3
  655.2 1.0 collective-permute-start
  656.2 2.4 convolution_convert_fusion.1
  658.6 1.0 slice_bitcast_fusion.6
  659.6 466.6 %reduce-scatter.2.cloned.1.call-done = bf16[8,2048]{1,0:T(8,128)(2,1)} async-done(((bf16[512,2048]{1,0:T(8,128)(2,1)}), bf16[8,2048]{1,0:T(8,128)(2,1)}) %reduce-scatter.2.cloned.1.call-update) | async-done | bytes 32784 | tf_op jit(solution)/shard_map/reduce_scatter | solution.py:45
  1126.2 67.2 %collective-permute-start.2 = (bf16[8,2048]{1,0:T(8,128)(2,1)}, bf16[8,2048]{1,0:T(8,128)(2,1)S(1)}, u32[]{:S(2)}, u32[]{:S(2)}) collective-permute-start(bf16[8,2048]{1,0:T(8,128)(2,1)} %reduce-scatter.2.cloned.1.call-done), channel_id=1, source_target_pairs={{0,448},{64,0},{128,64},{192,128},{256,192},{320,256},{384,320},{4... | collective-permute-start | bytes 98312 | tf_op jit(solution)/shard_map/ppermute | solution.py:13
  1193.4 3.2 fusion
  1196.5 0.0 collective-permute-done.1
  1196.5 0.0 collective-permute-done
  1196.5 0.0 collective-permute-done.2
  1196.6 1.1 fusion.5
  (1 shorter events, 0.0 us)
Async XLA Ops:
  7.2 596.4 %copy-start = (bf16[1,2048,128]{2,1,0:T(8,128)(2,1)S(1)}, bf16[1,2048,128]{2,1,0:T(8,128)(2,1)}, u32[]{:S(2)}) copy-start(bf16[1,2048,128]{2,1,0:T(8,128)(2,1)} %param.11) | copy-start | bytes 1572868
  7.2 593.6 %all-gather.2.cloned.1.call-start = ((), (), s32[]{:S(2)}) async-start(), calls=%async_computation.1 | async-start | bytes 4259840 | tf_op jit(solution)/shard_map/all_gather | solution.py:30
  11.8 1114.4 %reduce-scatter.2.cloned.1.call-start = ((), (), s32[]{:S(2)}) async-start(), calls=%async_computation.2 | async-start | bytes 2129920 | tf_op jit(solution)/shard_map/reduce_scatter | solution.py:45
  600.8 3.1 copy-start.4
  603.9 1.0 copy-start.1
  603.9 1.2 copy-start.2
  607.2 48.0 %copy-start.3 = (bf16[1,128,2048]{2,1,0:T(8,128)(2,1)S(1)}, bf16[1,128,2048]{2,1,0:T(8,128)(2,1)}, u32[]{:S(2)}) copy-start(bf16[1,128,2048]{2,1,0:T(8,128)(2,1)} %param.7) | copy-start | bytes 1572868
  607.3 589.3 %collective-permute-start.1 = (bf16[8,128]{1,0:T(8,128)(2,1)S(1)}, bf16[8,128]{1,0:T(8,128)(2,1)S(1)}, u32[]{:S(2)}, u32[]{:S(2)}) collective-permute-start(bf16[8,128]{1,0:T(8,128)(2,1)S(1)} %fusion.10), channel_id=1, source_target_pairs={{0,448},{64,0},{128,64},{192,128},{256,192},{320,256},{384,320},{4... | collective-permute-start | bytes 6152 | tf_op jit(solution)/shard_map/ppermute | solution.py:13
  655.2 541.3 %collective-permute-start = (bf16[128,2048]{1,0:T(8,128)(2,1)S(1)}, bf16[128,2048]{1,0:T(8,128)(2,1)S(1)}, u32[]{:S(2)}, u32[]{:S(2)}) collective-permute-start(bf16[128,2048]{1,0:T(8,128)(2,1)S(1)} %bitcast.47), channel_id=1, source_target_pairs={{0,448},{64,0},{128,64},{192,128},{256,192},{320,256},{384,320},{4... | collective-permute-start | bytes 1572872 | tf_op jit(solution)/shard_map/ppermute | solution.py:13
  1126.2 70.4 %collective-permute-start.2 = (bf16[8,2048]{1,0:T(8,128)(2,1)}, bf16[8,2048]{1,0:T(8,128)(2,1)S(1)}, u32[]{:S(2)}, u32[]{:S(2)}) collective-permute-start(bf16[8,2048]{1,0:T(8,128)(2,1)} %reduce-scatter.2.cloned.1.call-done), channel_id=1, source_target_pairs={{0,448},{64,0},{128,64},{192,128},{256,192},{320,256},{384,320},{4... | collective-permute-start | bytes 98312 | tf_op jit(solution)/shard_map/ppermute | solution.py:13
Sparse Core Ops, SparseCore 0:
  11.9 588.7 all-gather.1
  607.4 518.7 reduce-scatter.1
where the time goes:
time: 1200 us
  waiting for transfers between devices  1060 us (88%)
  starting transfers between devices  116 us (10%)
  matrix products  14.8 us (1%)
  between operations  14.1 us (1%)
    all_gather x1, waiting for transfers between devices, body(): lax.all_gather(jnp.stack([send_x, send_dy]), GROUP, axis=1, tiled=True)  589 us
    reduce_scatter x1, waiting for transfers between devices, body(): lax.psum_scatter(d_part.astype(jnp.bfloat16), GROUP, scatter_dimension=0,...  467 us
    ppermute x3, starting transfers between devices, shifted(): return lax.ppermute(value, axis, pairs)  116 us
  transfers between devices with their start and end apart: 5, of which 2 were waited for; matrix products, arithmetic and copies ran while one was open for 1% of the time, Pallas kernels for 0%

commit v1 on v0

--- a/solution.py
+++ b/solution.py
@@ -27,7 +27,12 @@
     send_dy = jnp.dot(match, grads, preferred_element_type=jnp.float32).astype(jnp.bfloat16)
     moved_grads = shifted(grads, "section", -1)
     moved_match = shifted(match, "section", -1)
-    rows = lax.all_gather(jnp.stack([send_x, send_dy]), GROUP, axis=1, tiled=True)
+    rows = jnp.concatenate(
+        lax.all_to_all(
+            jnp.stack([jnp.stack([send_x, send_dy])] * lax.axis_size(GROUP)), GROUP, 0, 0
+        ),
+        axis=1,
+    )
     x_rows, dy_rows = (rows[0], rows[1])
     w_both = jnp.concatenate([w_gate[0], w_up[0]], axis=1)
     both = jnp.dot(x_rows, w_both, preferred_element_type=jnp.float32)

time: 1200 us -> 780 us (0.65)
  waiting for transfers between devices: 1060 us -> 482 us
  blocking collectives: 0 us -> 198 us
  starting transfers between devices: 116 us -> 68.8 us
    all_gather x1 -> x0, waiting for transfers between devices: 589 us -> none  [body(): lax.all_gather(jnp.stack([send_x, send_dy]), GROUP, axis=1, tiled=True)]
    all_to_all x0 -> x1, blocking collectives: none -> 198 us  [body(): lax.all_to_all(jnp.stack([jnp.stack([send_x, send_dy])] * lax.axis_size(G...]
    ppermute x3, starting transfers between devices: 116 us -> 68.8 us  [shifted(): return lax.ppermute(value, axis, pairs)]
    reduce_scatter x1, waiting for transfers between devices: 467 us -> 482 us  [body(): lax.psum_scatter(d_part.astype(jnp.bfloat16), GROUP, scatter_dimension=0,...]
  transfers between devices with their start and end apart: 5 -> 4, of which waited for: 2 -> 1; matrix products, arithmetic and copies ran while one was open for 1% -> 1% of each run, Pallas kernels for 0% -> 0%
where the time goes in v1:
time: 780 us
  waiting for transfers between devices  482 us (62%)
  blocking collectives  198 us (25%)
  starting transfers between devices  68.8 us (9%)
  between operations  14.1 us (2%)
  matrix products  12.8 us (2%)
    reduce_scatter x1, waiting for transfers between devices, body(): lax.psum_scatter(d_part.astype(jnp.bfloat16), GROUP, scatter_dimension=0,...  482 us
    all_to_all x1, blocking collectives, body(): lax.all_to_all(jnp.stack([jnp.stack([send_x, send_dy])] * lax.axis_size(G...  198 us
    ppermute x3, starting transfers between devices, shifted(): return lax.ppermute(value, axis, pairs)  68.8 us
  transfers between devices with their start and end apart: 4, of which 1 were waited for; matrix products, arithmetic and copies ran while one was open for 1% of the time, Pallas kernels for 0%

profile of v1, /device:TPU:65, one launch (start us, length us, event | category | flops | bytes accessed | tf_op | source)
XLA Modules:
  0.0 780.0 jit_solution(6523241737964046626)
XLA Ops:
  7.2 0.0 copy-start
  7.2 0.0 reduce-scatter.2.cloned.1.call-start
  7.2 0.7 fusion.14
  7.9 0.1 select_reduce_fusion
  8.0 0.7 fusion.13
  8.7 1.2 fusion.1
  9.9 1.2 fusion.2
  11.2 0.5 stack.11
  11.7 0.0 copy-start.2
  11.7 0.0 copy-start.3
  11.7 197.7 %all_to_all.5 = bf16[64,2,8,2048]{3,2,1,0:T(8,128)(2,1)S(1)} all-to-all(bf16[64,2,8,2048]{3,2,1,0:T(8,128)(2,1)S(1)} %stack.11), channel_id=1, replica_groups=mesh['section'=8,'expert'=8,'dp'=8] {'expert','dp'}, dimensions={0} | all-to-all | bytes 8388608 | tf_op jit(solution)/shard_map/all_to_all | solution.py:31
  209.4 0.0 copy-start.1
  209.4 0.0 copy-done.2
  209.4 0.0 copy-done.3
  209.4 0.8 fusion.4
  210.2 1.2 copy-done.1
  211.4 0.0 copy-done
  211.4 0.9 multiply_convert_fusion.2
  212.2 2.1 convolution_convert_fusion
  214.3 0.0 copy-start.4
  214.3 0.0 reduce-scatter.2.cloned.1.call-update
  214.4 6.0 collective-permute-start.1
  220.3 0.0 copy-done.4
  220.3 1.0 collective-permute-start
  221.3 2.4 convolution_convert_fusion.1
  223.7 1.0 slice_bitcast_fusion.6
  224.7 482.2 %reduce-scatter.2.cloned.1.call-done = bf16[8,2048]{1,0:T(8,128)(2,1)} async-done(((bf16[512,2048]{1,0:T(8,128)(2,1)}), bf16[8,2048]{1,0:T(8,128)(2,1)}) %reduce-scatter.2.cloned.1.call-update) | async-done | bytes 32784 | tf_op jit(solution)/shard_map/reduce_scatter | solution.py:50
  707.0 61.8 %collective-permute-start.2 = (bf16[8,2048]{1,0:T(8,128)(2,1)}, bf16[8,2048]{1,0:T(8,128)(2,1)S(1)}, u32[]{:S(2)}, u32[]{:S(2)}) collective-permute-start(bf16[8,2048]{1,0:T(8,128)(2,1)} %reduce-scatter.2.cloned.1.call-done), channel_id=1, source_target_pairs={{0,448},{64,0},{128,64},{192,128},{256,192},{320,256},{384,320},{4... | collective-permute-start | bytes 98312 | tf_op jit(solution)/shard_map/ppermute | solution.py:13
  768.8 3.2 fusion
  772.0 0.0 collective-permute-done.1
  772.0 0.0 collective-permute-done
  772.0 0.0 collective-permute-done.2
  772.0 1.1 fusion.5
  (2 shorter events, 0.0 us)
Async XLA Ops:
  7.2 204.2 %copy-start = (bf16[1,2048,128]{2,1,0:T(8,128)(2,1)S(1)}, bf16[1,2048,128]{2,1,0:T(8,128)(2,1)}, u32[]{:S(2)}) copy-start(bf16[1,2048,128]{2,1,0:T(8,128)(2,1)} %param.11) | copy-start | bytes 1572868
  7.2 699.8 %reduce-scatter.2.cloned.1.call-start = ((), (), s32[]{:S(2)}) async-start(), calls=%async_computation.2 | async-start | bytes 2129920 | tf_op jit(solution)/shard_map/reduce_scatter | solution.py:50
  11.7 197.7 %copy-start.2 = (bf16[1,2048,128]{2,1,0:T(8,128)(2,1)S(1)}, bf16[1,2048,128]{2,1,0:T(8,128)(2,1)}, u32[]{:S(2)}) copy-start(bf16[1,2048,128]{2,1,0:T(8,128)(2,1)} %param.10) | copy-start | bytes 1572868
  11.7 197.7 %copy-start.3 = (bf16[1,2048,128]{2,1,0:T(8,128)(2,1)S(1)}, bf16[1,2048,128]{2,1,0:T(8,128)(2,1)}, u32[]{:S(2)}) copy-start(bf16[1,2048,128]{2,1,0:T(8,128)(2,1)} %param.9) | copy-start | bytes 1572868
  209.4 1.9 copy-start.1
  214.3 6.0 copy-start.4
  214.4 557.6 %collective-permute-start.1 = (bf16[8,128]{1,0:T(8,128)(2,1)S(1)}, bf16[8,128]{1,0:T(8,128)(2,1)S(1)}, u32[]{:S(2)}, u32[]{:S(2)}) collective-permute-start(bf16[8,128]{1,0:T(8,128)(2,1)S(1)} %fusion.10), channel_id=1, source_target_pairs={{0,448},{64,0},{128,64},{192,128},{256,192},{320,256},{384,320},{4... | collective-permute-start | bytes 6152 | tf_op jit(solution)/shard_map/ppermute | solution.py:13
  220.3 551.6 %collective-permute-start = (bf16[128,2048]{1,0:T(8,128)(2,1)S(1)}, bf16[128,2048]{1,0:T(8,128)(2,1)S(1)}, u32[]{:S(2)}, u32[]{:S(2)}) collective-permute-start(bf16[128,2048]{1,0:T(8,128)(2,1)S(1)} %bitcast.52), channel_id=1, source_target_pairs={{0,448},{64,0},{128,64},{192,128},{256,192},{320,256},{384,320},{4... | collective-permute-start | bytes 1572872 | tf_op jit(solution)/shard_map/ppermute | solution.py:13
  707.0 65.0 %collective-permute-start.2 = (bf16[8,2048]{1,0:T(8,128)(2,1)}, bf16[8,2048]{1,0:T(8,128)(2,1)S(1)}, u32[]{:S(2)}, u32[]{:S(2)}) collective-permute-start(bf16[8,2048]{1,0:T(8,128)(2,1)} %reduce-scatter.2.cloned.1.call-done), channel_id=1, source_target_pairs={{0,448},{64,0},{128,64},{192,128},{256,192},{320,256},{384,320},{4... | collective-permute-start | bytes 98312 | tf_op jit(solution)/shard_map/ppermute | solution.py:13
Sparse Core Ops, SparseCore 0:
  214.5 492.4 reduce-scatter.1
